TPU v7x, 512 devices: a whole 4x4x16 slice. The times are simulated.
512 devices in a mesh: sub: 64 (over z_lo, y, x), grp: 8 (over z_hi, core).
Axes of the slice: x: 4, y: 4, z: 16 (z_hi: 4, z_lo: 4; z = z_hi * 4 + z_lo), core: 2. Of those that a mesh axis runs over, the one named last changes fastest.
Arguments:
- residual: bfloat16 [8, 128, 6, 128, 256], P('grp', 'sub'), may hold values from -6 to 6
- sub_matrix: bfloat16 [8, 128, 12, 3, 128, 128], P('grp', 'sub'), may hold values from -0.15625 to 0.15625
- diag_inverse: bfloat16 [8, 128, 12, 128, 128], P('grp', 'sub'), may hold values from -0.5 to 0.5
- tile_cols: int32 [8, 128, 12, 3], P('grp', 'sub'), may hold values from 0 to 11
- outgoing_rows: int32 [8, 128, 2, 3], P('grp', 'sub'), may hold values from 0 to 5
- coarse_basis: bfloat16 [8, 128, 64, 6, 128], P('grp', 'sub'), may hold values from -0.21875 to 0.21875
- coarse_blocks: float32 [8, 128, 3, 64, 64], P('grp', 'sub'), may hold values from -0.375 to 0.375
- coarse_inverse: float32 [8, 128, 64, 64], P('grp', 'sub'), may hold values from -0.75 to 0.75
- coarse_links: int32 [8, 128, 2], P('grp', 'sub'), may hold values 0 or 1
Outputs:
- preconditioned: bfloat16 [8, 128, 6, 128, 256], P('grp', 'sub')
All inputs are finite; a program needn't handle non-finite values. No bound on the sum of `coarse_links` on one device may be relied on, other than what follows from the above.
Results may differ from a plain program's by a relative error of at most 0.0057.
Values may be sent and summed in bfloat16 or wider, within the bound.
A program may use at most 64 MiB of HBM per device.

v0:
```python
import jax
import jax.numpy as jnp
from jax import lax
from jax.sharding import PartitionSpec as P

SWEEPS = 2
CSWEEPS = 2


def extended(cells, sides, width):
    for axis, dim in sides:
        count = lax.axis_size(axis)
        ends = count - 1
        head = lax.slice_in_dim(cells, 0, width, axis=dim)
        tail = lax.slice_in_dim(cells, cells.shape[dim] - width, cells.shape[dim], axis=dim)
        cells = jnp.concatenate(
            [
                lax.ppermute(tail, axis, [(i, (i + 1) % count) for i in range(ends)]),
                cells,
                lax.ppermute(head, axis, [((i + 1) % count, i) for i in range(ends)]),
            ],
            axis=dim,
        )
    return cells


def received_rows(block, rows):
    return jnp.take(block, rows, axis=0)


def place_rows(rows, entry_values, count):
    marks = (rows[:, None] == jnp.arange(count, dtype=jnp.int32)[None, :]).astype(jnp.bfloat16)
    return jnp.einsum("on,otr->ntr", marks, entry_values, preferred_element_type=jnp.float32)


def coarse_update(right_hand_side, blocks, inverse, links, coarse_level, below, above):
    hi = lax.Precision.HIGHEST
    mult = lambda m, v: jnp.einsum("...ab,...br->...ar", m, v, precision=hi)
    defect = right_hand_side - mult(blocks[..., 0, :, :], coarse_level)
    defect = defect - links[..., 0][..., None, None] * mult(blocks[..., 1, :, :], below)
    defect = defect - links[..., 1][..., None, None] * mult(blocks[..., 2, :, :], above)
    return coarse_level + mult(inverse, defect)


def body(
    residual,
    sub_matrix,
    diag_inverse,
    tile_cols,
    outgoing_rows,
    coarse_basis,
    coarse_blocks,
    coarse_inverse,
    coarse_links,
):
    res = residual[0]
    rows = outgoing_rows[0]
    tiles = sub_matrix[0]
    inverse = diag_inverse[0]
    cols = tile_cols[0]
    basis = coarse_basis[0]
    owned = res.shape[1]
    lend = rows.shape[2]
    lent = jnp.concatenate(
        [received_rows(res[0], rows[0, 0]), received_rows(res[1], rows[1, 1])], 0
    )
    beside_all = extended(lent, (("sub", 0),), lend)
    first_ext = jnp.concatenate([beside_all[:lend], res[0], received_rows(res[1], rows[1, 0])], 0)
    second_ext = jnp.concatenate(
        [received_rows(res[0], rows[0, 1]), res[1], beside_all[3 * lend :]], 0
    )
    b_ext = jnp.stack([first_ext, second_ext], 0)
    b_f = b_ext.astype(jnp.float32)
    x = jnp.einsum("seij,sejr->seir", inverse, b_ext, preferred_element_type=jnp.float32).astype(
        jnp.bfloat16
    )
    for sweep in range(SWEEPS):
        picked = jax.vmap(received_rows)(x, cols)
        image = jnp.einsum("sekij,sekjr->seir", tiles, picked, preferred_element_type=jnp.float32)
        defect = (b_f - image).astype(jnp.bfloat16)
        x = (
            x.astype(jnp.float32)
            + jnp.einsum("seij,sejr->seir", inverse, defect, preferred_element_type=jnp.float32)
        ).astype(jnp.bfloat16)
    returned = jnp.concatenate([x[0, :lend], x[1, lend + owned :]], 0)
    back = extended(returned, (("sub", 0),), lend)
    first_fine = (
        x[0, lend : lend + owned].astype(jnp.float32)
        + place_rows(rows[0, 1], x[1, :lend], owned)
        + place_rows(rows[0, 0], back[:lend], owned)
    )
    second_fine = (
        x[1, lend : lend + owned].astype(jnp.float32)
        + place_rows(rows[1, 0], x[0, lend + owned :], owned)
        + place_rows(rows[1, 1], back[3 * lend :], owned)
    )
    fine = jnp.stack([first_fine, second_fine], 0)
    right_hand_side = jnp.einsum("scnt,sntr->scr", basis, res, preferred_element_type=jnp.float32)
    links = coarse_links.astype(jnp.float32)
    blocks = coarse_blocks[0]
    inverse_owned_block = coarse_inverse[0]
    links_own = links[0]
    coarse_level = jnp.einsum(
        "vpl,vlz->vpz", inverse_owned_block, right_hand_side, precision=lax.Precision.HIGHEST
    )
    for step in range(CSWEEPS):
        adjacent_block = extended(coarse_level.astype(jnp.bfloat16), (("grp", 0),), 2).astype(
            coarse_level.dtype
        )
        coarse_level = coarse_update(
            right_hand_side,
            blocks,
            inverse_owned_block,
            links_own,
            coarse_level,
            adjacent_block[:2],
            adjacent_block[4:],
        )
    level_b = coarse_level.astype(jnp.bfloat16)
    spread = jnp.einsum("scnt,scr->sntr", basis, level_b, preferred_element_type=jnp.float32)
    return (fine + spread).astype(jnp.bfloat16)[None]


def solution(mesh):
    in_specs = (
        P("grp", "sub", None, None, None),
        P("grp", "sub", None, None, None, None),
        P("grp", "sub", None, None, None),
        P("grp", "sub", None, None),
        P("grp", "sub", None, None),
        P("grp", "sub", None, None, None),
        P("grp", "sub", None, None, None),
        P("grp", "sub", None, None),
        P("grp", "sub", None),
    )
    out_specs = P("grp", "sub", None, None, None)
    return jax.shard_map(body, mesh=mesh, in_specs=in_specs, out_specs=out_specs, check_vma=False)
```

profile of v0, /device:TPU:416, one launch (start us, length us, event | category | flops | bytes accessed | tf_op | source)
XLA Modules:
  0.0 126.9 jit_solution(14653067432174616336)
XLA Ops:
  0.0 1.6 %convolution_bitcast_fusion = f32[2,64,256]{2,1,0:T(8,128)S(1)} fusion(bf16[1,2,6,128,256]{4,3,2,1,0:T(8,128)(2,1)} %param.13, bf16[1,2,64,6,128]{4,2,3,1,0:T(8,128)(2,1)} %param.18), kind=kOutput, calls=%fused_computation.30 | convolution fusion | flops 50331648 | bytes 1114112 | tf_op jit(solution)/shard_map/scnt,sntr->scr/dot_general | solution.py:98
  2.8 4.9 %collective-permute-start.5 = (bf16[2,64,256]{2,1,0:T(8,128)(2,1)S(1)}, bf16[2,64,256]{2,1,0:T(8,128)(2,1)}, u32[]{:S(2)}, u32[]{:S(2)}) collective-permute-start(bf16[2,64,256]{2,1,0:T(8,128)(2,1)S(1)} %convert_bitcast_fusion.1), channel_id=1, source_target_pairs={{1,0},{2,1},{3,2},{4,3},{5,4},{6,5},{7,6},{9,8},{10,9},{11,10},{12... | collective-permute-start | bytes 196616 | tf_op jit(solution)/shard_map/ppermute | solution.py:20
  7.7 1.9 %collective-permute-start.4 = (bf16[2,64,256]{2,1,0:T(8,128)(2,1)S(1)}, bf16[2,64,256]{2,1,0:T(8,128)(2,1)}, u32[]{:S(2)}, u32[]{:S(2)}) collective-permute-start(bf16[2,64,256]{2,1,0:T(8,128)(2,1)S(1)} %convert_bitcast_fusion.1), channel_id=1, source_target_pairs={{0,1},{1,2},{2,3},{3,4},{4,5},{5,6},{6,7},{8,9},{9,10},{10,11},{11... | collective-permute-start | bytes 196616 | tf_op jit(solution)/shard_map/ppermute | solution.py:18
  9.6 1.9 %fusion.84 = (bf16[1,1,6,128,256]{4,3,2,1,0:T(8,128)(2,1)S(1)}, bf16[1,1,6,128,256]{4,3,2,1,0:T(8,128)(2,1)}) fusion(bf16[1,2,6,128,256]{4,3,2,1,0:T(8,128)(2,1)} %param.13), kind=kLoop, calls=%fused_computation.127 | loop fusion | bytes 1572864 | tf_op jit(solution)/shard_map/slice | solution.py:65
  13.0 1.4 %broadcast_select_fusion.3 = bf16[3,128,256]{1,2,0:T(8,128)(2,1)} fusion(bf16[3,128,256]{1,2,0:T(8,128)(2,1)S(1)} %gather_fusion, pred[3]{0:T(512)(128)(4,1)} %get-tuple-element.9), kind=kLoop, calls=%fused_computation.74 | loop fusion | flops 98304 | bytes 393219 | tf_op jit(solution)/shard_map/jit(_take)/select_n | solution.py:28
  14.5 3.4 %collective-permute-start = (bf16[3,128,256]{1,2,0:T(8,128)(2,1)}, bf16[3,128,256]{1,2,0:T(8,128)(2,1)}, u32[]{:S(2)}, u32[]{:S(2)}) collective-permute-start(bf16[3,128,256]{1,2,0:T(8,128)(2,1)} %broadcast_select_fusion.3), channel_id=1, source_target_pairs={{0,8},{8,16},{16,24},{24,32},{32,40},{40,48},{48,56},{56,64},{64,7... | collective-permute-start | bytes 589832 | tf_op jit(solution)/shard_map/ppermute | solution.py:18
  19.7 1.2 gather_fusion.3
  21.0 1.7 %broadcast_select_fusion = bf16[3,128,256]{1,2,0:T(8,128)(2,1)} fusion(bf16[3,128,256]{1,2,0:T(8,128)(2,1)} %gather_fusion.3, pred[3]{0:T(512)(128)(4,1)S(1)} %get-tuple-element.29), kind=kLoop, calls=%fused_computation.71 | loop fusion | flops 98304 | bytes 393219 | tf_op jit(solution)/shard_map/jit(_take)/select_n | solution.py:28
  22.6 6.7 %collective-permute-start.1 = (bf16[3,128,256]{1,2,0:T(8,128)(2,1)}, bf16[3,128,256]{1,2,0:T(8,128)(2,1)}, u32[]{:S(2)}, u32[]{:S(2)}) collective-permute-start(bf16[3,128,256]{1,2,0:T(8,128)(2,1)} %broadcast_select_fusion), channel_id=1, source_target_pairs={{8,0},{16,8},{24,16},{32,24},{40,32},{48,40},{56,48},{64,56},{72,6... | collective-permute-start | bytes 589832 | tf_op jit(solution)/shard_map/ppermute | solution.py:20
  30.6 1.2 gather_fusion.1
  32.5 1.2 gather_fusion.2
  41.0 7.1 %collective-permute-start.7 = (bf16[2,64,256]{2,1,0:T(8,128)(2,1)S(1)}, bf16[2,64,256]{2,1,0:T(8,128)(2,1)S(1)}, u32[]{:S(2)}, u32[]{:S(2)}) collective-permute-start(bf16[2,64,256]{2,1,0:T(8,128)(2,1)S(1)} %convert_bitcast_fusion), channel_id=1, source_target_pairs={{1,0},{2,1},{3,2},{4,3},{5,4},{6,5},{7,6},{9,8},{10,9},{11,10},{12... | collective-permute-start | bytes 196616 | tf_op jit(solution)/shard_map/ppermute | solution.py:20
  48.5 2.1 %collective-permute-start.6 = (bf16[2,64,256]{2,1,0:T(8,128)(2,1)S(1)}, bf16[2,64,256]{2,1,0:T(8,128)(2,1)S(1)}, u32[]{:S(2)}, u32[]{:S(2)}) collective-permute-start(bf16[2,64,256]{2,1,0:T(8,128)(2,1)S(1)} %convert_bitcast_fusion), channel_id=1, source_target_pairs={{0,1},{1,2},{2,3},{3,4},{4,5},{5,6},{6,7},{8,9},{9,10},{10,11},{11... | collective-permute-start | bytes 196616 | tf_op jit(solution)/shard_map/ppermute | solution.py:18
  50.8 8.1 %collective-permute-done.6 = bf16[2,64,256]{2,1,0:T(8,128)(2,1)S(1)} collective-permute-done((bf16[2,64,256]{2,1,0:T(8,128)(2,1)S(1)}, bf16[2,64,256]{2,1,0:T(8,128)(2,1)S(1)}, u32[]{:S(2)}, u32[]{:S(2)}) %collective-permute-start.6) | collective-permute-done | bytes 65568 | tf_op jit(solution)/shard_map/ppermute | solution.py:18
  60.4 1.3 maximum_bitcast_fusion.1
  62.6 1.8 %fusion.17 = bf16[2,12,128,256]{2,3,1,0:T(8,128)(2,1)} fusion(bf16[1,2,12,128,128]{4,3,2,1,0:T(8,128)(2,1)S(1)} %copy-done.13, bf16[1,12,128,256]{2,3,1,0:T(8,128)(2,1)S(1)} %maximum_bitcast_fusion.1, bf16[1,12,128,256]{2,3,1,0:T(8,128)(2,1)S(1)} %maximum_bitcast_fusion), kind=kOutput, calls=%fused_computation.28 | convolution fusion | flops 202899456 | bytes 3932160 | tf_op jit(solution)/shard_map/seij,sejr->seir/dot_general | solution.py:74
  64.4 8.4 %gather_fusion.4 = bf16[72,128,256]{1,2,0:T(8,128)(2,1)} fusion(bf16[2,12,128,256]{2,3,1,0:T(8,128)(2,1)} %fusion.17, s32[72]{0:T(128)S(1)} %reshape.93), kind=kCustom, calls=%fused_computation.1.clone | custom fusion | bytes 9437760 | tf_op jit(solution)/shard_map/vmap(jit(_take))/gather | solution.py:28
  72.8 6.3 %fusion.9 = bf16[2,12,128,256]{2,3,1,0:T(8,128)(2,1)} fusion(bf16[2,12,128,256]{2,3,1,0:T(8,128)(2,1)} %fusion.17, bf16[2,12,3,128,256]{3,4,2,1,0:T(8,128)(2,1)} %bitcast.202, pred[2,12,3]{2,1,0:T(8,128)(4,1)S(1)} %copy.27, bf16[1,2,12,3,128,128]{5,4,3,2,1,0:T(8,128)(2,1)S(1)} %copy-done, bf16[1,2,12,128,128]{4,3,2,1,0:T(8,128)(2,1)} %param.15, ...), kind=kOutput, calls=%fused_computation.19 | convolution fusion | flops 813170688 | bytes 12582984 | tf_op jit(solution)/shard_map/seij,sejr->seir/dot_general | solution.py:83
  79.1 8.3 %gather_fusion.5 = bf16[72,128,256]{1,2,0:T(8,128)(2,1)} fusion(bf16[2,12,128,256]{2,3,1,0:T(8,128)(2,1)} %fusion.9, s32[72]{0:T(128)S(1)} %reshape.93), kind=kCustom, calls=%fused_computation.5.clone | custom fusion | bytes 9437760 | tf_op jit(solution)/shard_map/vmap(jit(_take))/gather | solution.py:28
  87.4 6.3 %fusion.8 = bf16[2,12,128,256]{2,3,1,0:T(8,128)(2,1)} fusion(bf16[2,12,128,256]{2,3,1,0:T(8,128)(2,1)} %fusion.9, bf16[2,12,3,128,256]{3,4,2,1,0:T(8,128)(2,1)} %bitcast.201, pred[2,12,3]{2,1,0:T(8,128)(4,1)S(1)} %copy.27, bf16[1,2,12,3,128,128]{5,4,3,2,1,0:T(8,128)(2,1)S(1)} %copy-done, bf16[1,2,12,128,128]{4,3,2,1,0:T(8,128)(2,1)} %param.15, ...), kind=kOutput, calls=%fused_computation.17 | convolution fusion | flops 813170688 | bytes 12582984 | tf_op jit(solution)/shard_map/seij,sejr->seir/dot_general | solution.py:83
  93.8 2.1 %slice_bitcast_fusion.5 = (bf16[3,128,256]{1,2,0:T(8,128)(2,1)S(1)}, bf16[3,128,256]{1,2,0:T(8,128)(2,1)}, bf16[3,128,256]{1,2,0:T(8,128)(2,1)}, bf16[3,128,256]{1,2,0:T(8,128)(2,1)}) fusion(bf16[2,12,128,256]{2,3,1,0:T(8,128)(2,1)} %fusion.8), kind=kLoop, calls=%fused_computation.68 | loop fusion | bytes 1572864 | tf_op jit(solution)/shard_map/squeeze | solution.py:89
  95.9 2.0 %collective-permute-start.2 = (bf16[3,128,256]{1,2,0:T(8,128)(2,1)}, bf16[3,128,256]{1,2,0:T(8,128)(2,1)}, u32[]{:S(2)}, u32[]{:S(2)}) collective-permute-start(bf16[3,128,256]{1,2,0:T(8,128)(2,1)} %get-tuple-element.22), channel_id=1, source_target_pairs={{0,8},{8,16},{16,24},{24,32},{32,40},{40,48},{48,56},{56,64},{64,7... | collective-permute-start | bytes 589832 | tf_op jit(solution)/shard_map/ppermute | solution.py:18
  97.9 8.4 %collective-permute-start.3 = (bf16[3,128,256]{1,2,0:T(8,128)(2,1)}, bf16[3,128,256]{1,2,0:T(8,128)(2,1)}, u32[]{:S(2)}, u32[]{:S(2)}) collective-permute-start(bf16[3,128,256]{1,2,0:T(8,128)(2,1)} %get-tuple-element.20), channel_id=1, source_target_pairs={{8,0},{16,8},{24,16},{32,24},{40,32},{48,40},{56,48},{64,56},{72,6... | collective-permute-start | bytes 589832 | tf_op jit(solution)/shard_map/ppermute | solution.py:20
  107.2 1.4 %fusion.62 = f32[6,128,256]{2,0,1:T(8,128)S(1)} fusion(bf16[3,128,256]{2,0,1:T(4,128)(2,1)} %copy.31, s32[3]{0:T(128)S(1)} %copy-done.12), kind=kOutput, calls=%fused_computation.100 | convolution fusion | flops 1179666 | bytes 983052 | tf_op jit(solution)/shard_map/on,otr->ntr/dot_general | solution.py:33
  109.8 1.8 %copy.35 = bf16[3,128,256]{2,0,1:T(4,128)(2,1)} copy(bf16[3,128,256]{1,2,0:T(8,128)(2,1)} %get-tuple-element.21) | data formatting | bytes 393216 | tf_op jit(solution)/shard_map/squeeze | solution.py:94
  111.6 1.4 %fusion.68 = f32[6,128,256]{2,0,1:T(8,128)S(1)} fusion(bf16[3,128,256]{2,0,1:T(4,128)(2,1)} %copy.35, s32[3]{0:T(128)S(1)} %copy-done.11), kind=kOutput, calls=%fused_computation.104 | convolution fusion | flops 1179666 | bytes 983052 | tf_op jit(solution)/shard_map/on,otr->ntr/dot_general | solution.py:33
  112.9 1.3 copy.36
  114.2 1.8 %copy.33 = bf16[3,128,256]{2,0,1:T(4,128)(2,1)} copy(bf16[3,128,256]{1,2,0:T(8,128)(2,1)} %collective-permute-done.2) | data formatting | bytes 393216 | tf_op jit(solution)/shard_map/ppermute | solution.py:18
  116.0 1.4 %fusion.65 = f32[6,128,256]{2,0,1:T(8,128)S(1)} fusion(bf16[3,128,256]{2,0,1:T(4,128)(2,1)} %copy.33, s32[3]{0:T(128)S(1)} %copy-done.10), kind=kOutput, calls=%fused_computation.102 | convolution fusion | flops 1179666 | bytes 983052 | tf_op jit(solution)/shard_map/on,otr->ntr/dot_general | solution.py:33
  118.6 1.8 %copy.37 = bf16[3,128,256]{2,0,1:T(4,128)(2,1)} copy(bf16[3,128,256]{1,2,0:T(8,128)(2,1)} %collective-permute-done.3) | data formatting | bytes 393216 | tf_op jit(solution)/shard_map/ppermute | solution.py:20
  120.4 1.4 %fusion.71 = f32[6,128,256]{2,0,1:T(8,128)S(1)} fusion(bf16[3,128,256]{2,0,1:T(4,128)(2,1)} %copy.37, s32[3]{0:T(128)S(1)} %copy-done.9), kind=kOutput, calls=%fused_computation.106 | convolution fusion | flops 1179666 | bytes 983052 | tf_op jit(solution)/shard_map/on,otr->ntr/dot_general | solution.py:33
  123.0 2.3 %fusion.50 = (f32[1,6,128,256]{2,3,1,0:T(8,128)S(1)}, f32[1,6,128,256]{2,3,1,0:T(8,128)S(1)}) fusion(f32[6,128,256]{1,2,0:T(8,128)} %copy.34, f32[6,128,256]{1,2,0:T(8,128)} %copy.32, bf16[2,12,128,256]{2,3,1,0:T(8,128)(2,1)} %fusion.8, f32[6,128,256]{1,2,0:T(8,128)} %copy.38, f32[6,128,256]{1,2,0:T(8,128)} %copy.36), kind=kLoop, calls=%fused_computation.58 | loop fusion | flops 1179648 | bytes 5505024 | tf_op jit(solution)/shard_map/stack | solution.py:97
  (70 shorter events, 22.5 us)
Async XLA Ops:
  0.0 72.8 %copy-start = (bf16[1,2,12,3,128,128]{5,4,3,2,1,0:T(8,128)(2,1)S(1)}, bf16[1,2,12,3,128,128]{5,4,3,2,1,0:T(8,128)(2,1)}, u32[]{:S(2)}) copy-start(bf16[1,2,12,3,128,128]{5,4,3,2,1,0:T(8,128)(2,1)} %param.14) | copy-start | bytes 7077892
  0.0 11.6 %copy-start.8 = (s32[1,2,2,3]{3,2,1,0:T(2,128)S(1)}, s32[1,2,2,3]{3,2,1,0:T(2,128)}, u32[]{:S(2)}) copy-start(s32[1,2,2,3]{3,2,1,0:T(2,128)} %param.17) | copy-start | bytes 148
  2.8 26.5 %copy-start.7 = (s32[1,2,12,3]{2,1,3,0:T(2,128)S(1)}, s32[1,2,12,3]{2,1,3,0:T(2,128)}, u32[]{:S(2)}) copy-start(s32[1,2,12,3]{2,1,3,0:T(2,128)} %param.16) | copy-start | bytes 868
  2.8 35.8 %collective-permute-start.5 = (bf16[2,64,256]{2,1,0:T(8,128)(2,1)S(1)}, bf16[2,64,256]{2,1,0:T(8,128)(2,1)}, u32[]{:S(2)}, u32[]{:S(2)}) collective-permute-start(bf16[2,64,256]{2,1,0:T(8,128)(2,1)S(1)} %convert_bitcast_fusion.1), channel_id=1, source_target_pairs={{1,0},{2,1},{3,2},{4,3},{5,4},{6,5},{7,6},{9,8},{10,9},{11,10},{12... | collective-permute-start | bytes 196616 | tf_op jit(solution)/shard_map/ppermute | solution.py:20
  7.7 31.9 %collective-permute-start.4 = (bf16[2,64,256]{2,1,0:T(8,128)(2,1)S(1)}, bf16[2,64,256]{2,1,0:T(8,128)(2,1)}, u32[]{:S(2)}, u32[]{:S(2)}) collective-permute-start(bf16[2,64,256]{2,1,0:T(8,128)(2,1)S(1)} %convert_bitcast_fusion.1), channel_id=1, source_target_pairs={{0,1},{1,2},{2,3},{3,4},{4,5},{5,6},{6,7},{8,9},{9,10},{10,11},{11... | collective-permute-start | bytes 196616 | tf_op jit(solution)/shard_map/ppermute | solution.py:18
  13.0 27.7 %copy-start.6 = (f32[1,2,64,64]{3,2,1,0:T(8,128)S(1)}, f32[1,2,64,64]{3,2,1,0:T(8,128)}, u32[]{:S(2)}) copy-start(f32[1,2,64,64]{3,2,1,0:T(8,128)} %param.20) | copy-start | bytes 98308
  14.5 44.9 %collective-permute-start = (bf16[3,128,256]{1,2,0:T(8,128)(2,1)}, bf16[3,128,256]{1,2,0:T(8,128)(2,1)}, u32[]{:S(2)}, u32[]{:S(2)}) collective-permute-start(bf16[3,128,256]{1,2,0:T(8,128)(2,1)} %broadcast_select_fusion.3), channel_id=1, source_target_pairs={{0,8},{8,16},{16,24},{24,32},{32,40},{40,48},{48,56},{56,64},{64,7... | collective-permute-start | bytes 589832 | tf_op jit(solution)/shard_map/ppermute | solution.py:18
  22.6 37.8 %collective-permute-start.1 = (bf16[3,128,256]{1,2,0:T(8,128)(2,1)}, bf16[3,128,256]{1,2,0:T(8,128)(2,1)}, u32[]{:S(2)}, u32[]{:S(2)}) collective-permute-start(bf16[3,128,256]{1,2,0:T(8,128)(2,1)} %broadcast_select_fusion), channel_id=1, source_target_pairs={{8,0},{16,8},{24,16},{32,24},{40,32},{48,40},{56,48},{64,56},{72,6... | collective-permute-start | bytes 589832 | tf_op jit(solution)/shard_map/ppermute | solution.py:20
  35.4 12.8 %copy-start.4 = (f32[1,2,3,64,64]{4,3,2,1,0:T(8,128)S(1)}, f32[1,2,3,64,64]{4,3,2,1,0:T(8,128)}, u32[]{:S(2)}) copy-start(f32[1,2,3,64,64]{4,3,2,1,0:T(8,128)} %param.19) | copy-start | bytes 294916
  41.0 21.6 %copy-start.13 = (bf16[1,2,12,128,128]{4,3,2,1,0:T(8,128)(2,1)S(1)}, bf16[1,2,12,128,128]{4,3,2,1,0:T(8,128)(2,1)}, u32[]{:S(2)}) copy-start(bf16[1,2,12,128,128]{4,3,2,1,0:T(8,128)(2,1)} %param.15) | copy-start | bytes 2359300
  41.0 9.5 %collective-permute-start.7 = (bf16[2,64,256]{2,1,0:T(8,128)(2,1)S(1)}, bf16[2,64,256]{2,1,0:T(8,128)(2,1)S(1)}, u32[]{:S(2)}, u32[]{:S(2)}) collective-permute-start(bf16[2,64,256]{2,1,0:T(8,128)(2,1)S(1)} %convert_bitcast_fusion), channel_id=1, source_target_pairs={{1,0},{2,1},{3,2},{4,3},{5,4},{6,5},{7,6},{9,8},{10,9},{11,10},{12... | collective-permute-start | bytes 196616 | tf_op jit(solution)/shard_map/ppermute | solution.py:20
  48.5 10.5 %collective-permute-start.6 = (bf16[2,64,256]{2,1,0:T(8,128)(2,1)S(1)}, bf16[2,64,256]{2,1,0:T(8,128)(2,1)S(1)}, u32[]{:S(2)}, u32[]{:S(2)}) collective-permute-start(bf16[2,64,256]{2,1,0:T(8,128)(2,1)S(1)} %convert_bitcast_fusion), channel_id=1, source_target_pairs={{0,1},{1,2},{2,3},{3,4},{4,5},{5,6},{6,7},{8,9},{9,10},{10,11},{11... | collective-permute-start | bytes 196616 | tf_op jit(solution)/shard_map/ppermute | solution.py:18
  60.4 1.3 %copy-start.1 = (bf16[1,12,128,256]{2,3,1,0:T(8,128)(2,1)}, bf16[1,12,128,256]{2,3,1,0:T(8,128)(2,1)S(1)}, u32[]{:S(2)}) copy-start(bf16[1,12,128,256]{2,3,1,0:T(8,128)(2,1)S(1)} %maximum_bitcast_fusion) | copy-start | bytes 2359300
  61.7 0.9 copy-start.3
  64.4 8.4 %copy-start.2 = (bf16[1,12,128,256]{2,3,1,0:T(8,128)(2,1)S(1)}, bf16[1,12,128,256]{2,3,1,0:T(8,128)(2,1)}, u32[]{:S(2)}) copy-start(bf16[1,12,128,256]{2,3,1,0:T(8,128)(2,1)} %copy-done.1) | copy-start | bytes 2359300
  87.4 19.7 %copy-start.12 = (s32[3]{0:T(128)S(1)}, s32[3]{0:T(128)}, u32[]{:S(2)}) copy-start(s32[3]{0:T(128)} %get-tuple-element.25) | copy-start | bytes 40
  95.9 15.7 %copy-start.11 = (s32[3]{0:T(128)S(1)}, s32[3]{0:T(128)}, u32[]{:S(2)}) copy-start(s32[3]{0:T(128)} %get-tuple-element.27) | copy-start | bytes 40
  95.9 18.3 %collective-permute-start.2 = (bf16[3,128,256]{1,2,0:T(8,128)(2,1)}, bf16[3,128,256]{1,2,0:T(8,128)(2,1)}, u32[]{:S(2)}, u32[]{:S(2)}) collective-permute-start(bf16[3,128,256]{1,2,0:T(8,128)(2,1)} %get-tuple-element.22), channel_id=1, source_target_pairs={{0,8},{8,16},{16,24},{24,32},{32,40},{40,48},{48,56},{56,64},{64,7... | collective-permute-start | bytes 589832 | tf_op jit(solution)/shard_map/ppermute | solution.py:18
  97.9 20.7 %collective-permute-start.3 = (bf16[3,128,256]{1,2,0:T(8,128)(2,1)}, bf16[3,128,256]{1,2,0:T(8,128)(2,1)}, u32[]{:S(2)}, u32[]{:S(2)}) collective-permute-start(bf16[3,128,256]{1,2,0:T(8,128)(2,1)} %get-tuple-element.20), channel_id=1, source_target_pairs={{8,0},{16,8},{24,16},{32,24},{40,32},{48,40},{56,48},{64,56},{72,6... | collective-permute-start | bytes 589832 | tf_op jit(solution)/shard_map/ppermute | solution.py:20
  109.8 6.2 %copy-start.10 = (s32[3]{0:T(128)S(1)}, s32[3]{0:T(128)}, u32[]{:S(2)}) copy-start(s32[3]{0:T(128)} %get-tuple-element.26) | copy-start | bytes 40
  114.2 6.2 %copy-start.9 = (s32[3]{0:T(128)S(1)}, s32[3]{0:T(128)}, u32[]{:S(2)}) copy-start(s32[3]{0:T(128)} %get-tuple-element.28) | copy-start | bytes 40
  123.0 2.3 %copy-start.5 = (bf16[1,2,64,6,128]{4,2,3,1,0:T(8,128)(2,1)S(1)}, bf16[1,2,64,6,128]{4,2,3,1,0:T(8,128)(2,1)}, u32[]{:S(2)}) copy-start(bf16[1,2,64,6,128]{4,2,3,1,0:T(8,128)(2,1)} %param.18) | copy-start | bytes 589828
where the time goes:
time: 128 us; the launch traced here: 127 us
  local copies, waits for them, and re-layouts  42.2 us (33%)
  starting transfers between devices  36.5 us (29%)
  matrix products  27.4 us (21%)
  other arithmetic  12.2 us (10%)
  waiting for transfers between devices  8.16 us (6%)
    ppermute x4, starting transfers between devices, extended(): lax.ppermute(head, axis, [((i + 1) % count, i) for i in range(ends)])  27 us
    gather x8, local copies, waits for them, and re-layouts, received_rows(): return jnp.take(block, rows, axis=0)  22.6 us
    dot_general x2, matrix products, body(): jnp.einsum('seij,sejr->seir', inverse, defect, preferred_element_type=jnp...  12.7 us
    ppermute x4, starting transfers between devices, extended(): lax.ppermute(tail, axis, [(i, (i + 1) % count) for i in range(ends)])  9.45 us
    ppermute x4, waiting for transfers between devices, extended(): lax.ppermute(tail, axis, [(i, (i + 1) % count) for i in range(ends)])  8.15 us
    dot_general x4, matrix products, place_rows(): jnp.einsum('on,otr->ntr', marks, entry_values, preferred_element_type=jnp...  5.41 us
    dot_general x4, local copies, waits for them, and re-layouts, place_rows(): jnp.einsum('on,otr->ntr', marks, entry_values, preferred_element_type=jnp...  4.96 us
    dot_general x8, matrix products, coarse_update(): mult = lambda m, v: jnp.einsum('...ab,...br->...ar', m, v, precision=hi)  4.42 us
  transfers between devices with their start and end apart: 8, of which 1 were waited for; matrix products, arithmetic and copies ran while one was open for 28% of the time, Pallas kernels for 0%

commit v1 on v0

v1 whole, which is shorter than its diff:
```python
import jax
import jax.numpy as jnp
from jax import lax
from jax.experimental import pallas as pl
from jax.experimental.pallas import tpu as pltpu
from jax.sharding import PartitionSpec as P

MESH = pl.DeviceIdType.MESH
BF = jnp.bfloat16
F32 = jnp.float32
OWN, EXT, LEND, TILE, RHS, COARSE = 6, 12, 3, 128, 256, 64
WIDTH = 128
CHUNKS = RHS // WIDTH


def mm(a, b):
    return jnp.dot(a, b, preferred_element_type=F32)


def split(a):
    hi = a.astype(BF)
    return hi, (a - hi.astype(F32)).astype(BF)


def cols_of(c):
    return slice(c * WIDTH, (c + 1) * WIDTH)


def kernel(
    res_h, mat_h, inv_h, cols_h, rows_h, bas_h, blk_h, cinv_h, links_h,
    out,
    cols, rows, links, res, mat, inv, bas, blk, cinv, bast,
    x0f, x0, x1, x2, pre,
    lsend, lrecv, rsend, rrecv,
    qa, ia, xq, lv0, lv, csend, lev_b,
    load_sem, ls_sem, lr_sem, rs_sem, rr_sem, cs_sem, cr_sem,
):
    sub = lax.axis_index("sub")
    grp = lax.axis_index("grp")
    subs = lax.axis_size("sub")
    grps = lax.axis_size("grp")
    has_r, has_l = sub < subs - 1, sub > 0
    has_u, has_d = grp < grps - 1, grp > 0
    right, left = {"sub": sub + 1}, {"sub": sub - 1}
    up, down = {"grp": grp + 1}, {"grp": grp - 1}

    barrier = pltpu.get_barrier_semaphore()
    sides = ((has_r, right), (has_l, left), (has_u, up), (has_d, down))
    for has, device in sides:
        @pl.when(has)
        def _():
            pl.semaphore_signal(barrier, 1, device_id=device, device_id_type=MESH)

    loads = [
        pltpu.make_async_copy(src, dst, load_sem.at[i])
        for i, (src, dst) in enumerate(
            ((rows_h, rows), (res_h.at[0], res), (bas_h.at[0], bas), (cinv_h.at[0], cinv), (blk_h.at[0], blk),
             (links_h, links), (inv_h.at[0], inv), (mat_h.at[0], mat), (cols_h, cols))
        )
    ]
    for copy in loads:
        copy.start()

    def lend_copy(d, c):
        return pltpu.make_async_remote_copy(
            src_ref=lsend.at[d, c], dst_ref=lrecv.at[d, c], send_sem=ls_sem.at[d, c],
            recv_sem=lr_sem.at[d, c], device_id=(right, left)[d], device_id_type=MESH)

    def back_copy(d, c):
        return pltpu.make_async_remote_copy(
            src_ref=rsend.at[d, c], dst_ref=rrecv.at[d, c], send_sem=rs_sem.at[d, c],
            recv_sem=rr_sem.at[d, c], device_id=(right, left)[d], device_id_type=MESH)

    def level_copy(step, d):
        at = (1 + d) * COARSE
        return pltpu.make_async_remote_copy(
            src_ref=csend.at[step], dst_ref=xq.at[step, :, at : at + COARSE],
            send_sem=cs_sem.at[step, d], recv_sem=cr_sem.at[step, d],
            device_id=(up, down)[d], device_id_type=MESH)

    goes = (has_r, has_l)
    comes = (has_l, has_r)
    climbs = (has_u, has_d)
    falls = (has_d, has_u)

    for d in range(2):
        @pl.when(jnp.logical_not(comes[d]))
        def _():
            lrecv[d] = jnp.zeros(lrecv.shape[1:], BF)
            rrecv[d] = jnp.zeros(rrecv.shape[1:], BF)

        @pl.when(jnp.logical_not(falls[d]))
        def _():
            for step in range(2):
                at = (1 + d) * COARSE
                xq[step, :, at : at + COARSE] = jnp.zeros((2, COARSE, RHS), BF)

    loads[0].wait()
    loads[1].wait()
    for c in range(CHUNKS):
        for o in range(LEND):
            lsend[0, c, o] = res[1, rows[0, 1, 1, o], :, cols_of(c)]
            lsend[1, c, o] = res[0, rows[0, 0, 0, o], :, cols_of(c)]
    count = sum(has.astype(jnp.int32) for has, _ in sides)
    pl.semaphore_wait(barrier, count)
    for c in range(CHUNKS):
        for d in range(2):
            @pl.when(goes[d])
            def _():
                lend_copy(d, c).start()

    loads[2].wait()
    loads[3].wait()
    for s in range(2):
        hi, lo = split(cinv[s])
        ia[s, :COARSE] = hi
        ia[s, COARSE:] = lo
        basis = jnp.concatenate([bas[s, n] for n in range(OWN)], axis=1)
        rhs = mm(basis, res[s].reshape(OWN * TILE, RHS))
        rhi, rlo = split(rhs)
        both = mm(ia[s], rhi)
        level = both[:COARSE] + both[COARSE:] + mm(hi, rlo)
        lv0[s] = level
        lhi, llo = split(level)
        csend[0, s] = lhi
        xq[0, s, :COARSE] = lhi
        xq[0, s, 3 * COARSE :] = llo
    for d in range(2):
        @pl.when(climbs[d])
        def _():
            level_copy(0, d).start()

    loads[4].wait()
    loads[5].wait()
    for s in range(2):
        for n in range(OWN):
            bast[s, n * TILE : (n + 1) * TILE, :] = bas[s, n].T
        for j in range(3):
            q = jnp.dot(cinv[s], blk[s, j], precision=lax.Precision.HIGHEST, preferred_element_type=F32)
            if j:
                q = q * links[0, s, j - 1].astype(F32)
            hi, lo = split(q)
            at = j * COARSE
            qa[s, :COARSE, at : at + COARSE] = hi
            qa[s, COARSE:, at : at + COARSE] = lo
            if j == 0:
                qa[s, :COARSE, 3 * COARSE :] = hi
                qa[s, COARSE:, 3 * COARSE :] = jnp.zeros_like(lo)

    loads[6].wait()

    def first(s, e, b, c=None):
        y = mm(inv[s, e], b)
        where = slice(None) if c is None else cols_of(c)
        x0f[s, e, :, where] = y
        x0[s, e, :, where] = y.astype(BF)

    for s in range(2):
        for n in range(OWN):
            first(s, LEND + n, res[s, n])
    for o in range(LEND):
        first(0, LEND + OWN + o, res[1, rows[0, 1, 0, o]])
        first(1, o, res[0, rows[0, 0, 1, o]])

    loads[7].wait()
    loads[8].wait()
    for s in range(2):
        for e in range(EXT):
            tiles = jnp.concatenate([mat[s, e, k] for k in range(3)], axis=1)
            q = mm(inv[s, e], tiles).astype(BF)
            for k in range(3):
                mat[s, e, k] = q[:, k * TILE : (k + 1) * TILE]

    def swept(s, e, c, x):
        tiles = jnp.concatenate([mat[s, e, k] for k in range(3)], axis=1)
        picked = jnp.concatenate([x[s, cols[0, k, s, e], :, cols_of(c)] for k in range(3)], axis=0)
        y = x0f[s, e, :, cols_of(c)] + x[s, e, :, cols_of(c)].astype(F32) - mm(tiles, picked)
        return y.astype(BF)

    def level_step(step):
        for d in range(2):
            @pl.when(falls[d])
            def _():
                level_copy(step, d).wait_recv()
        for s in range(2):
            both = mm(qa[s], xq[step, s])
            old = lv0[s] if step == 0 else lv[s]
            level = old + lv0[s] - (both[:COARSE] + both[COARSE:])
            if step == 0:
                lv[s] = level
                lhi, llo = split(level)
                csend[1, s] = lhi
                xq[1, s, :COARSE] = lhi
                xq[1, s, 3 * COARSE :] = llo
            else:
                lev_b[s] = level.astype(BF)
        if step == 0:
            for d in range(2):
                @pl.when(climbs[d])
                def _():
                    level_copy(1, d).start()

    for c in range(CHUNKS):
        for d in range(2):
            @pl.when(comes[d])
            def _():
                lend_copy(d, c).wait_recv()
        for o in range(LEND):
            first(0, o, lrecv[0, c, o], c)
            first(1, LEND + OWN + o, lrecv[1, c, o], c)
        for s in range(2):
            for e in range(EXT):
                x1[s, e, :, cols_of(c)] = swept(s, e, c, x0)
        for o in range(LEND):
            rsend[0, c, o] = swept(1, LEND + OWN + o, c, x1)
            rsend[1, c, o] = swept(0, o, c, x1)
        for d in range(2):
            @pl.when(goes[d])
            def _():
                back_copy(d, c).start()
        if c == 0:
            level_step(0)
    for c in range(CHUNKS):
        for e in range(LEND, EXT):
            x2[0, e, :, cols_of(c)] = swept(0, e, c, x1)
        for e in range(LEND + OWN):
            x2[1, e, :, cols_of(c)] = swept(1, e, c, x1)
    level_step(1)

    for s in range(2):
        spread = mm(bast[s], lev_b[s])
        for n in range(OWN):
            y = x2[s, LEND + n].astype(F32) + spread[n * TILE : (n + 1) * TILE]
            for o in range(LEND):
                mark = (rows[0, s, 1 - s, o] == n).astype(F32)
                y = y + mark * x2[1 - s, (0 if s == 0 else LEND + OWN) + o].astype(F32)
            pre[s, n] = y

    for c in range(CHUNKS):
        for d in range(2):
            @pl.when(comes[d])
            def _():
                back_copy(d, c).wait_recv()
        for s in range(2):
            for n in range(OWN):
                y = pre[s, n, :, cols_of(c)]
                for o in range(LEND):
                    mark = (rows[0, s, s, o] == n).astype(F32)
                    y = y + mark * rrecv[s, c, o].astype(F32)
                out[0, s, n, :, cols_of(c)] = y.astype(BF)

    for d in range(2):
        @pl.when(goes[d])
        def _():
            for c in range(CHUNKS):
                lend_copy(d, c).wait_send()
                back_copy(d, c).wait_send()

        @pl.when(climbs[d])
        def _():
            for step in range(2):
                level_copy(step, d).wait_send()


def body(*args):
    residual, mat, inv, cols, rows, basis, blocks, coarse_inverse, links = args
    args = (residual, mat, inv, jnp.transpose(cols, (0, 3, 1, 2)), rows,
            jnp.transpose(basis, (0, 1, 3, 2, 4)), blocks, coarse_inverse, links)
    vm, sm, dma = pltpu.VMEM, pltpu.SMEM, pltpu.SemaphoreType.DMA
    ext = (2, EXT, TILE, RHS)
    moved = (2, CHUNKS, LEND, TILE, WIDTH)
    return pl.pallas_call(
        kernel,
        out_shape=pltpu.VMEM(residual.shape, BF),
        in_specs=[pl.BlockSpec(memory_space=pl.ANY)] * 9,
        out_specs=pl.BlockSpec(memory_space=pltpu.VMEM),
        scratch_shapes=[
            sm((1, 3, 2, EXT), jnp.int32), sm((1, 2, 2, LEND), jnp.int32), sm((1, 2, 2), jnp.int32),
            vm((2, OWN, TILE, RHS), BF), vm((2, EXT, 3, TILE, TILE), BF), vm((2, EXT, TILE, TILE), BF),
            vm((2, OWN, COARSE, TILE), BF), vm((2, 3, COARSE, COARSE), F32), vm((2, COARSE, COARSE), F32),
            vm((2, OWN * TILE, COARSE), BF),
            vm(ext, F32), vm(ext, BF), vm(ext, BF), vm(ext, BF), vm((2, OWN, TILE, RHS), F32),
            vm(moved, BF), vm(moved, BF), vm(moved, BF), vm(moved, BF),
            vm((2, 2 * COARSE, 4 * COARSE), BF), vm((2, 2 * COARSE, COARSE), BF),
            vm((2, 2, 4 * COARSE, RHS), BF), vm((2, COARSE, RHS), F32), vm((2, COARSE, RHS), F32),
            vm((2, 2, COARSE, RHS), BF), vm((2, COARSE, RHS), BF),
            dma((9,)), dma((2, CHUNKS)), dma((2, CHUNKS)), dma((2, CHUNKS)), dma((2, CHUNKS)),
            dma((2, 2)), dma((2, 2)),
        ],
        compiler_params=pltpu.CompilerParams(
            collective_id=0, has_side_effects=True, vmem_limit_bytes=58 * 1024 * 1024
        ),
        cost_estimate=pl.CostEstimate(flops=2_000_000_000, bytes_accessed=5_000_000, transcendentals=0),
        name="schwarz",
    )(*args)


def solution(mesh):
    in_specs = (
        P("grp", "sub", None, None, None),
        P("grp", "sub", None, None, None, None),
        P("grp", "sub", None, None, None),
        P("grp", "sub", None, None),
        P("grp", "sub", None, None),
        P("grp", "sub", None, None, None),
        P("grp", "sub", None, None, None),
        P("grp", "sub", None, None),
        P("grp", "sub", None),
    )
    out_specs = P("grp", "sub", None, None, None)
    return jax.shard_map(body, mesh=mesh, in_specs=in_specs, out_specs=out_specs, check_vma=False)
```

time: 128 us -> 28.1 us (0.22)
  the two profiles are of different devices: /device:TPU:416 before, /device:TPU:161 now
where the time goes in v1:
time: 28.1 us; the launch traced here: 28 us
  Pallas kernels  27.1 us (96%)
  local copies, waits for them, and re-layouts  0.88 us (3%)
    pallas_call x1, Pallas kernels, body(): pl.pallas_call(kernel, out_shape=pltpu.VMEM(residual.shape, BF), in_specs...  27.1 us
    unnamed x1, local copies, waits for them, and re-layouts  0.88 us

profile of v1, /device:TPU:161, one launch (start us, length us, event | category | flops | bytes accessed | tf_op | source)
XLA Modules:
  0.0 28.0 jit_solution(3271362182975713433)
XLA Ops:
  0.0 27.1 %schwarz.1 = bf16[1,2,6,128,256]{4,3,2,1,0:T(8,128)(2,1)S(1)} custom-call(bf16[1,2,6,128,256]{4,3,2,1,0:T(8,128)(2,1)} %res_h.1, bf16[1,2,12,3,128,128]{5,4,3,2,1,0:T(8,128)(2,1)} %mat_h.1, bf16[1,2,12,128,128]{4,3,2,1,0:T(8,128)(2,1)} %inv_h.1, s32[1,3,2,12]{3,2,1,0:T(2,128)} %bitcast.3, s32[1,2,2,3]{3,2,1,0:T(2,128)} %rows_h.1, ...), custom_call_target="tpu_custom_call" | custom-call | flops 2000000000 | bytes 5000000 | tf_op jit(solution)/shard_map/schwarz/pallas_call | solution.py:272
  27.1 0.9 %copy.11 = bf16[1,2,6,128,256]{4,3,2,1,0:T(8,128)(2,1)} copy(bf16[1,2,6,128,256]{4,3,2,1,0:T(8,128)(2,1)S(1)} %schwarz.1) | data formatting | bytes 1572864

commit v2 on v1

--- a/solution.py
+++ b/solution.py
@@ -58,18 +58,18 @@
              (links_h, links), (inv_h.at[0], inv), (mat_h.at[0], mat), (cols_h, cols))
         )
     ]
-    for copy in loads:
+    for copy in loads[:2]:
         copy.start()
 
     def lend_copy(d, c):
         return pltpu.make_async_remote_copy(
             src_ref=lsend.at[d, c], dst_ref=lrecv.at[d, c], send_sem=ls_sem.at[d, c],
-            recv_sem=lr_sem.at[d, c], device_id=(right, left)[d], device_id_type=MESH)
+            recv_sem=lr_sem.at[d, c], device_id={"sub": sub + 1 - 2 * d}, device_id_type=MESH)
 
     def back_copy(d, c):
         return pltpu.make_async_remote_copy(
             src_ref=rsend.at[d, c], dst_ref=rrecv.at[d, c], send_sem=rs_sem.at[d, c],
-            recv_sem=rr_sem.at[d, c], device_id=(right, left)[d], device_id_type=MESH)
+            recv_sem=rr_sem.at[d, c], device_id={"sub": sub + 1 - 2 * d}, device_id_type=MESH)
 
     def level_copy(step, d):
         at = (1 + d) * COARSE
@@ -97,18 +97,12 @@
 
     loads[0].wait()
     loads[1].wait()
+    for copy in loads[2:]:
+        copy.start()
     for c in range(CHUNKS):
         for o in range(LEND):
             lsend[0, c, o] = res[1, rows[0, 1, 1, o], :, cols_of(c)]
             lsend[1, c, o] = res[0, rows[0, 0, 0, o], :, cols_of(c)]
-    count = sum(has.astype(jnp.int32) for has, _ in sides)
-    pl.semaphore_wait(barrier, count)
-    for c in range(CHUNKS):
-        for d in range(2):
-            @pl.when(goes[d])
-            def _():
-                lend_copy(d, c).start()
-
     loads[2].wait()
     loads[3].wait()
     for s in range(2):
@@ -125,6 +119,14 @@
         csend[0, s] = lhi
         xq[0, s, :COARSE] = lhi
         xq[0, s, 3 * COARSE :] = llo
+    count = sum(has.astype(jnp.int32) for has, _ in sides)
+    pl.semaphore_wait(barrier, count)
+    for c in range(CHUNKS):
+        for d in range(2):
+            @pl.when(goes[d])
+            def _():
+                lend_copy(d, c).start()
+
     for d in range(2):
         @pl.when(climbs[d])
         def _():
@@ -149,22 +151,24 @@
 
     loads[6].wait()
 
-    def first(s, e, b, c=None):
+    def first(s, e, b):
         y = mm(inv[s, e], b)
-        where = slice(None) if c is None else cols_of(c)
-        x0f[s, e, :, where] = y
-        x0[s, e, :, where] = y.astype(BF)
-
-    for s in range(2):
+        for c in range(CHUNKS):
+            x0f[c, s, e] = y[:, cols_of(c)]
+            x0[c, s, e] = y[:, cols_of(c)].astype(BF)
+
+    @pl.loop(0, 2)
+    def _(s):
         for n in range(OWN):
             first(s, LEND + n, res[s, n])
-    for o in range(LEND):
-        first(0, LEND + OWN + o, res[1, rows[0, 1, 0, o]])
-        first(1, o, res[0, rows[0, 0, 1, o]])
+        for o in range(LEND):
+            first(s, (1 - s) * (LEND + OWN) + o, res[1 - s, rows[0, 1 - s, s, o]])
 
     loads[7].wait()
     loads[8].wait()
-    for s in range(2):
+
+    @pl.loop(0, 2)
+    def _(s):
         for e in range(EXT):
             tiles = jnp.concatenate([mat[s, e, k] for k in range(3)], axis=1)
             q = mm(inv[s, e], tiles).astype(BF)
@@ -173,8 +177,8 @@
 
     def swept(s, e, c, x):
         tiles = jnp.concatenate([mat[s, e, k] for k in range(3)], axis=1)
-        picked = jnp.concatenate([x[s, cols[0, k, s, e], :, cols_of(c)] for k in range(3)], axis=0)
-        y = x0f[s, e, :, cols_of(c)] + x[s, e, :, cols_of(c)].astype(F32) - mm(tiles, picked)
+        picked = jnp.concatenate([x[c, s, cols[0, k, s, e]] for k in range(3)], axis=0)
+        y = x0f[c, s, e] + x[c, s, e].astype(F32) - mm(tiles, picked)
         return y.astype(BF)
 
     def level_step(step):
@@ -200,50 +204,60 @@
                 def _():
                     level_copy(1, d).start()
 
-    for c in range(CHUNKS):
-        for d in range(2):
-            @pl.when(comes[d])
+    early = (sub % 4 == 0).astype(jnp.int32)
+
+    def beside(s):
+        return jnp.where(s == 0, has_l, has_r)
+
+    def solve(s, c):
+        @pl.when(beside(s))
+        def _():
+            lend_copy(s, c).wait_recv()
+        edge = s * (LEND + OWN)
+        for o in range(LEND):
+            y = mm(inv[s, edge + o], lrecv[s, c, o])
+            x0f[c, s, edge + o] = y
+            x0[c, s, edge + o] = y.astype(BF)
+        for e in range(EXT):
+            x1[c, s, e] = swept(s, e, c, x0)
+        for o in range(LEND):
+            rsend[1 - s, c, o] = swept(s, edge + o, c, x1)
+
+        @pl.when(beside(s))
+        def _():
+            back_copy(1 - s, c).start()
+
+    def finish(s, c):
+        kept = (1 - s) * LEND
+        for e in range(LEND + OWN):
+            x2[c, s, kept + e] = swept(s, kept + e, c, x1)
+
+    pl.loop(0, CHUNKS)(lambda c: solve(early, c))
+    pl.loop(0, CHUNKS)(lambda c: finish(early, c))
+    level_step(0)
+    pl.loop(0, CHUNKS)(lambda c: solve(1 - early, c))
+    pl.loop(0, CHUNKS)(lambda c: finish(1 - early, c))
+    level_step(1)
+
+    @pl.loop(0, 2)
+    def _(s):
+        spread = mm(bast[s], lev_b[s])
+        for c in range(CHUNKS):
+            for n in range(OWN):
+                y = x2[c, s, LEND + n].astype(F32) + spread[n * TILE : (n + 1) * TILE, cols_of(c)]
+                for o in range(LEND):
+                    mark = (rows[0, s, 1 - s, o] == n).astype(F32)
+                    y = y + mark * x2[c, 1 - s, s * (LEND + OWN) + o].astype(F32)
+                pre[c, s, n] = y
+
+    for i in range(2):
+        s = early if i == 0 else 1 - early
+        for c in range(CHUNKS):
+            @pl.when(beside(s))
             def _():
-                lend_copy(d, c).wait_recv()
-        for o in range(LEND):
-            first(0, o, lrecv[0, c, o], c)
-            first(1, LEND + OWN + o, lrecv[1, c, o], c)
-        for s in range(2):
-            for e in range(EXT):
-                x1[s, e, :, cols_of(c)] = swept(s, e, c, x0)
-        for o in range(LEND):
-            rsend[0, c, o] = swept(1, LEND + OWN + o, c, x1)
-            rsend[1, c, o] = swept(0, o, c, x1)
-        for d in range(2):
-            @pl.when(goes[d])
-            def _():
-                back_copy(d, c).start()
-        if c == 0:
-            level_step(0)
-    for c in range(CHUNKS):
-        for e in range(LEND, EXT):
-            x2[0, e, :, cols_of(c)] = swept(0, e, c, x1)
-        for e in range(LEND + OWN):
-            x2[1, e, :, cols_of(c)] = swept(1, e, c, x1)
-    level_step(1)
-
-    for s in range(2):
-        spread = mm(bast[s], lev_b[s])
-        for n in range(OWN):
-            y = x2[s, LEND + n].astype(F32) + spread[n * TILE : (n + 1) * TILE]
-            for o in range(LEND):
-                mark = (rows[0, s, 1 - s, o] == n).astype(F32)
-                y = y + mark * x2[1 - s, (0 if s == 0 else LEND + OWN) + o].astype(F32)
-            pre[s, n] = y
-
-    for c in range(CHUNKS):
-        for d in range(2):
-            @pl.when(comes[d])
-            def _():
-                back_copy(d, c).wait_recv()
-        for s in range(2):
+                back_copy(s, c).wait_recv()
             for n in range(OWN):
-                y = pre[s, n, :, cols_of(c)]
+                y = pre[c, s, n]
                 for o in range(LEND):
                     mark = (rows[0, s, s, o] == n).astype(F32)
                     y = y + mark * rrecv[s, c, o].astype(F32)
@@ -267,7 +281,7 @@
     args = (residual, mat, inv, jnp.transpose(cols, (0, 3, 1, 2)), rows,
             jnp.transpose(basis, (0, 1, 3, 2, 4)), blocks, coarse_inverse, links)
     vm, sm, dma = pltpu.VMEM, pltpu.SMEM, pltpu.SemaphoreType.DMA
-    ext = (2, EXT, TILE, RHS)
+    ext = (CHUNKS, 2, EXT, TILE, WIDTH)
     moved = (2, CHUNKS, LEND, TILE, WIDTH)
     return pl.pallas_call(
         kernel,
@@ -279,7 +293,7 @@
             vm((2, OWN, TILE, RHS), BF), vm((2, EXT, 3, TILE, TILE), BF), vm((2, EXT, TILE, TILE), BF),
             vm((2, OWN, COARSE, TILE), BF), vm((2, 3, COARSE, COARSE), F32), vm((2, COARSE, COARSE), F32),
             vm((2, OWN * TILE, COARSE), BF),
-            vm(ext, F32), vm(ext, BF), vm(ext, BF), vm(ext, BF), vm((2, OWN, TILE, RHS), F32),
+            vm(ext, F32), vm(ext, BF), vm(ext, BF), vm(ext, BF), vm((CHUNKS, 2, OWN, TILE, WIDTH), F32),
             vm(moved, BF), vm(moved, BF), vm(moved, BF), vm(moved, BF),
             vm((2, 2 * COARSE, 4 * COARSE), BF), vm((2, 2 * COARSE, COARSE), BF),
             vm((2, 2, 4 * COARSE, RHS), BF), vm((2, COARSE, RHS), F32), vm((2, COARSE, RHS), F32),

time: 28.1 us -> 27.6 us (0.982)
  the two profiles are of different devices: /device:TPU:161 before, /device:TPU:63 now
where the time goes in v2:
time: 27.6 us; the launch traced here: 27.5 us
  Pallas kernels  26.6 us (96%)
  local copies, waits for them, and re-layouts  0.88 us (3%)
    pallas_call x1, Pallas kernels, body(): pl.pallas_call(kernel, out_shape=pltpu.VMEM(residual.shape, BF), in_specs...  26.6 us
    unnamed x1, local copies, waits for them, and re-layouts  0.88 us

profile of v2, /device:TPU:63, one launch (start us, length us, event | category | flops | bytes accessed | tf_op | source)
XLA Modules:
  0.0 27.5 jit_solution(3249099856769596939)
XLA Ops:
  0.0 26.6 %schwarz.1 = bf16[1,2,6,128,256]{4,3,2,1,0:T(8,128)(2,1)S(1)} custom-call(bf16[1,2,6,128,256]{4,3,2,1,0:T(8,128)(2,1)} %res_h.1, bf16[1,2,12,3,128,128]{5,4,3,2,1,0:T(8,128)(2,1)} %mat_h.1, bf16[1,2,12,128,128]{4,3,2,1,0:T(8,128)(2,1)} %inv_h.1, s32[1,3,2,12]{3,2,1,0:T(2,128)} %bitcast.3, s32[1,2,2,3]{3,2,1,0:T(2,128)} %rows_h.1, ...), custom_call_target="tpu_custom_call" | custom-call | flops 2000000000 | bytes 5000000 | tf_op jit(solution)/shard_map/schwarz/pallas_call | solution.py:286
  26.6 0.9 %copy.11 = bf16[1,2,6,128,256]{4,3,2,1,0:T(8,128)(2,1)} copy(bf16[1,2,6,128,256]{4,3,2,1,0:T(8,128)(2,1)S(1)} %schwarz.1) | data formatting | bytes 1572864
